TPU v7x, 256 devices: a whole 4x4x8 slice. The times are simulated.
256 devices in a mesh: dp: 8 (over z_lo, core), expert: 32 (over z_hi, y, x).
Axes of the slice: x: 4, y: 4, z: 8 (z_hi: 2, z_lo: 4; z = z_hi * 4 + z_lo), core: 2. Of those that a mesh axis runs over, the one named last changes fastest.
Arguments:
- tokens: bfloat16 [65536, 1280], P(('dp', 'expert')), may hold values from -24 to 24
- router: bfloat16 [1280, 64], replicated, may hold values from -11 to 11
- w_in: bfloat16 [64, 1280, 4096], P('expert', None, 'dp'), may hold values from -0.15625 to 0.15625
- w_out: bfloat16 [64, 4096, 1280], P('expert', 'dp'), may hold values from -0.09375 to 0.09375
- out_grad: bfloat16 [65536, 1280], P(('dp', 'expert')), may hold values from -6 to 6
Outputs:
- token_grad: bfloat16 [65536, 1280], P(('dp', 'expert'))
- router_grad: float32 [1280, 64], replicated
- w_in_grad: bfloat16 [64, 1280, 4096], P('expert', None, 'dp')
- w_out_grad: bfloat16 [64, 4096, 1280], P('expert', 'dp')
All inputs are finite; a program needn't handle non-finite values.
Results may differ from a plain program's by a relative error of at most 0.012.
Values may be sent and summed in bfloat16 or wider, within the bound.
A program may use at most 64 MiB of HBM per device.

v0:
```python
import jax
import jax.numpy as jnp
from jax import lax
from jax.sharding import Mesh
from jax.sharding import PartitionSpec as P

M = 256
DP = ("dp_0", "dp_1")
DP_EXPERT = ("dp_0", "dp_1", "expert")


def laid_out(blocks, dim):
    blocks = jnp.moveaxis(blocks, 0, dim)
    lengths = blocks.shape
    return blocks.reshape(*lengths[:dim], lengths[dim] * lengths[dim + 1], *lengths[dim + 2 :])


def gather_in_order(value, axes, order):
    blocks = value
    for k in order:
        blocks = lax.all_gather(blocks, axes[k])
    done = order[::-1]
    back = [done.index(k) for k in range(len(axes))]
    blocks = blocks.transpose(*back, *range(len(axes), blocks.ndim))
    return blocks.reshape(-1, *value.shape)


def gathered_by_axis(value, axes, order, dim):
    return laid_out(gather_in_order(value, axes, order), dim)


def activate(values):
    return jax.nn.gelu(values, approximate=True)


def to_experts(slot_rows):
    placed = lax.all_to_all(slot_rows, "expert", split_axis=1, concat_axis=0, tiled=True)
    return gathered_by_axis(placed, DP, (0, 1), 0)


def to_owners(partial_value):
    summed = lax.psum_scatter(partial_value, DP, scatter_dimension=0, tiled=True).astype(
        jnp.bfloat16
    )
    return lax.all_to_all(summed, "expert", split_axis=0, concat_axis=1, tiled=True)


def local(tokens, router, w_in, w_out, out_grad):
    images = tokens.shape[0] // M
    feature = tokens.shape[1]
    inputs = tokens.reshape(images, M, feature)
    grads = out_grad.reshape(images, M, feature)
    logits = jnp.einsum("bmd,de->bme", inputs, router, preferred_element_type=jnp.float32)
    dispatch = jax.nn.softmax(logits, axis=1)
    combine = jax.nn.softmax(logits, axis=2)
    dispatch_b = dispatch.astype(jnp.bfloat16)
    combine_b = combine.astype(jnp.bfloat16)
    slots = jnp.einsum(
        "bme,bmd->bed", dispatch_b, inputs, preferred_element_type=jnp.float32
    ).astype(jnp.bfloat16)
    slot_rows = to_experts(slots)
    hidden = jnp.einsum("red,edf->ref", slot_rows, w_in, preferred_element_type=jnp.float32)
    active, pull = jax.vjp(activate, hidden)
    active_b = active.astype(jnp.bfloat16)
    partial_value = jnp.einsum("ref,efd->red", active_b, w_out, preferred_element_type=jnp.float32)
    slot_out = to_owners(partial_value)
    slot_grad = jnp.einsum(
        "bme,bmd->bed", combine_b, grads, preferred_element_type=jnp.float32
    ).astype(jnp.bfloat16)
    grad_rows = to_experts(slot_grad)
    active_grad = jnp.einsum("red,efd->ref", grad_rows, w_out, preferred_element_type=jnp.float32)
    second_grad = jnp.einsum(
        "ref,red->efd", active_b, grad_rows, preferred_element_type=jnp.float32
    ).astype(jnp.bfloat16)
    hidden_grad = pull(active_grad)[0].astype(jnp.bfloat16)
    first_grad = jnp.einsum(
        "red,ref->edf", slot_rows, hidden_grad, preferred_element_type=jnp.float32
    ).astype(jnp.bfloat16)
    input_partial = jnp.einsum(
        "ref,edf->red", hidden_grad, w_in, preferred_element_type=jnp.float32
    )
    slot_in_grad = to_owners(input_partial)
    combine_grad = jnp.einsum("bmd,bed->bme", grads, slot_out, preferred_element_type=jnp.float32)
    dispatch_grad = jnp.einsum(
        "bmd,bed->bme", inputs, slot_in_grad, preferred_element_type=jnp.float32
    )
    logit_grad = combine * (combine_grad - jnp.sum(combine_grad * combine, axis=2, keepdims=True))
    logit_grad = logit_grad + dispatch * (
        dispatch_grad - jnp.sum(dispatch_grad * dispatch, axis=1, keepdims=True)
    )
    logit_b = logit_grad.astype(jnp.bfloat16)
    token_grad = jnp.einsum(
        "bme,bed->bmd", dispatch_b, slot_in_grad, preferred_element_type=jnp.float32
    )
    token_grad = token_grad + jnp.einsum(
        "bme,de->bmd", logit_b, router, preferred_element_type=jnp.float32
    )
    router_part = jnp.einsum("bmd,bme->de", inputs, logit_b, preferred_element_type=jnp.float32)
    router_grad = lax.psum(router_part, DP_EXPERT)
    return (
        token_grad.astype(jnp.bfloat16).reshape(images * M, feature),
        router_grad,
        first_grad,
        second_grad,
    )


def solution(mesh):
    split = Mesh(mesh.devices.reshape(4, 2, mesh.shape["expert"]), ("dp_0", "dp_1", "expert"))
    placed = (
        P(DP_EXPERT, None),
        P(),
        P("expert", None, DP),
        P("expert", DP, None),
        P(DP_EXPERT, None),
    )
    return jax.shard_map(
        local,
        mesh=split,
        in_specs=placed,
        out_specs=(P(DP_EXPERT, None), P(), P("expert", None, DP), P("expert", DP, None)),
        check_vma=False,
    )
```

profile of v0, /device:TPU:1, one launch (start us, length us, event | category | flops | bytes accessed | tf_op | source)
XLA Modules:
  0.0 484.6 jit_solution(391703074439383236)
XLA Ops:
  7.2 0.0 copy-start
  7.2 0.0 all-gather.7.cloned.1.call-start
  7.2 1.7 fusion.21
  9.0 0.2 fusion.13
  9.2 1.4 fusion.2
  10.5 0.3 copy.45
  10.8 0.5 broadcast.53
  11.3 1.6 reduce.16
  12.9 0.1 reshape.119
  13.0 25.8 %all_to_all.42 = bf16[32,2,1280]{2,1,0:T(2,128)(2,1)S(1)} all-to-all(bf16[32,2,1280]{2,1,0:T(2,128)(2,1)S(1)} %reshape.119), channel_id=1, replica_groups=mesh['dp_0'=4,'dp_1'=2,'expert'=32] {'expert'}, dimensions={0} | all-to-all | bytes 327680 | tf_op jit(solution)/shard_map/all_to_all | solution.py:37
  38.8 0.1 reshape.120
  38.9 0.9 bitcast_reduce_fusion.1
  39.8 0.1 all_to_all.15
  39.9 15.2 %all_gather.23 = bf16[4,32,2,1280]{3,1,2,0:T(8,128)(2,1)} all-gather(bf16[1,32,2,1280]{3,1,2,0:T(8,128)(2,1)S(1)} %copy.33), channel_id=1, replica_groups=mesh['dp_0'=4,'dp_1'=2,'expert'=32] {'dp_0'}, dimensions={0}, use_global_device_ids=true | all-gather | bytes 819200 | tf_op jit(solution)/shard_map/all_gather | solution.py:21
  55.2 0.0 all-gather.7.cloned.1.call-update
  55.2 0.0 all-gather.5.cloned.1.call-start
  55.3 1.3 fusion.1
  56.6 0.3 copy.46
  56.8 1.6 reduce.17
  58.4 0.1 reshape.121
  58.5 15.0 %all_to_all.43 = bf16[32,2,1280]{2,1,0:T(2,128)(2,1)S(1)} all-to-all(bf16[32,2,1280]{2,1,0:T(2,128)(2,1)S(1)} %reshape.121), channel_id=1, replica_groups=mesh['dp_0'=4,'dp_1'=2,'expert'=32] {'expert'}, dimensions={0} | all-to-all | bytes 327680 | tf_op jit(solution)/shard_map/all_to_all | solution.py:37
  73.5 0.1 reshape.122
  73.6 0.9 bitcast_reduce_fusion
  74.5 0.1 all_to_all.13
  74.6 14.8 %all_gather.20 = bf16[4,32,2,1280]{3,1,2,0:T(8,128)(2,1)} all-gather(bf16[1,32,2,1280]{3,1,2,0:T(8,128)(2,1)S(1)} %copy.30), channel_id=1, replica_groups=mesh['dp_0'=4,'dp_1'=2,'expert'=32] {'dp_0'}, dimensions={0}, use_global_device_ids=true | all-gather | bytes 819200 | tf_op jit(solution)/shard_map/all_gather | solution.py:21
  89.4 0.0 all-gather.5.cloned.1.call-update
  89.4 0.0 reduce-scatter.3.cloned.1.call-start
  89.5 0.0 all-gather.7.cloned.1.call-done
  89.5 2.5 copy.34
  92.0 15.6 %all-gather.5.cloned.1.call-done = bf16[8,32,2,1280]{3,1,2,0:T(8,128)(2,1)} async-done(((bf16[4,32,2,1280]{3,1,2,0:T(8,128)(2,1)}), bf16[8,32,2,1280]{3,1,2,0:T(8,128)(2,1)}) %all-gather.5.cloned.1.call-update) | async-done | bytes 1310736 | tf_op jit(solution)/shard_map/all_gather | solution.py:21
  107.6 1.5 copy.31
  109.1 0.2 copy-done.1
  109.3 0.8 convolution_bitcast_fusion.3
  110.1 1.6 copy-done.5
  111.7 1.3 fusion.9
  113.1 0.8 copy-done.6
  113.8 2.4 convolution_bitcast_fusion.1
  116.2 0.0 reduce-scatter.3.cloned.1.call-update
  116.3 0.0 reduce-scatter.5.cloned.1.call-start
  116.3 4.5 convolution_bitcast_fusion
  120.8 0.0 reduce-scatter.5.cloned.1.call-update
  120.8 4.1 convolution_convert_fusion
  124.9 32.3 %reduce-scatter.3.cloned.1.call-done = f32[32,2,1280]{2,0,1:T(8,128)} async-done(((f32[256,2,1280]{2,0,1:T(8,128)}), f32[32,2,1280]{2,0,1:T(8,128)}) %reduce-scatter.3.cloned.1.call-update) | async-done | bytes 327696 | tf_op jit(solution)/shard_map/reduce_scatter | solution.py:42
  157.2 1.0 convert_element_type.53
  158.2 0.8 copy.35
  159.0 11.1 %all-to-all-start.2 = ((bf16[32,2,1280]{2,1,0:T(2,128)(2,1)}), bf16[32,2,1280]{2,1,0:T(2,128)(2,1)S(1)}, u32[]{:S(2)}, u32[]{:S(2)}) async-start(bf16[32,2,1280]{2,1,0:T(2,128)(2,1)} %copy.35), calls=%async_computation.3 | async-start | bytes 327680 | tf_op jit(solution)/shard_map/all_to_all | solution.py:45
  170.1 3.9 convolution_convert_fusion.1
  174.0 29.4 %reduce-scatter.5.cloned.1.call-done = f32[32,2,1280]{2,0,1:T(8,128)} async-done(((f32[256,2,1280]{2,0,1:T(8,128)}), f32[32,2,1280]{2,0,1:T(8,128)}) %reduce-scatter.5.cloned.1.call-update) | async-done | bytes 327696 | tf_op jit(solution)/shard_map/reduce_scatter | solution.py:42
  203.4 1.0 convert_element_type.55
  204.4 0.8 copy.36
  205.3 10.4 %all-to-all-start.3 = ((bf16[32,2,1280]{2,1,0:T(2,128)(2,1)}), bf16[32,2,1280]{2,1,0:T(2,128)(2,1)}, u32[]{:S(2)}, u32[]{:S(2)}) async-start(bf16[32,2,1280]{2,1,0:T(2,128)(2,1)} %copy.36), calls=%async_computation.5 | async-start | bytes 327680 | tf_op jit(solution)/shard_map/all_to_all | solution.py:45
  215.6 0.0 all-reduce.2.cloned.1.call-start
  215.7 1.0 reshape.113
  216.7 1.0 convolution_bitcast_fusion.5
  217.6 1.5 fusion.15
  219.1 7.9 %all-to-all-done.3 = bf16[32,2,1280]{2,1,0:T(2,128)(2,1)} async-done(((bf16[32,2,1280]{2,1,0:T(2,128)(2,1)}), bf16[32,2,1280]{2,1,0:T(2,128)(2,1)}, u32[]{:S(2)}, u32[]{:S(2)}) %all-to-all-start.3) | async-done | bytes 163872 | tf_op jit(solution)/shard_map/all_to_all | solution.py:45
  227.0 1.6 reshape.114
  228.7 1.6 multiply_reduce_fusion.1
  230.3 0.6 copy-done.9
  230.9 1.9 convolution_bitcast_fusion.2
  232.7 0.0 all-reduce.2.cloned.1.call-update
  232.8 2.7 fusion
  235.4 240.9 %all-reduce.2.cloned.1.call-done = f32[1280,64]{0,1:T(8,128)} async-done(((f32[1280,64]{0,1:T(8,128)}), f32[1280,64]{0,1:T(8,128)}) %all-reduce.2.cloned.1.call-update) | async-done | bytes 327696 | tf_op jit(solution)/shard_map/psum | solution.py:99
  476.3 1.7 copy.50
  (18 shorter events, 0.1 us)
Async XLA Ops:
  7.2 101.9 %copy-start = (bf16[2,1280,512]{2,1,0:T(8,128)(2,1)S(1)}, bf16[2,1280,512]{2,1,0:T(8,128)(2,1)}, u32[]{:S(2)}) copy-start(bf16[2,1280,512]{2,1,0:T(8,128)(2,1)} %param.7) | copy-start | bytes 7864324
  7.2 82.3 %all-gather.7.cloned.1.call-start = ((), (), s32[]{:S(2)}) async-start(), calls=%async_computation.10 | async-start | bytes 1966080 | tf_op jit(solution)/shard_map/all_gather | solution.py:21
  55.2 52.3 %all-gather.5.cloned.1.call-start = ((), (), s32[]{:S(2)}) async-start(), calls=%async_computation.9 | async-start | bytes 1966080 | tf_op jit(solution)/shard_map/all_gather | solution.py:21
  89.4 67.8 %reduce-scatter.3.cloned.1.call-start = ((), (), s32[]{:S(2)}) async-start(), calls=%async_computation.6 | async-start | bytes 2949120 | tf_op jit(solution)/shard_map/reduce_scatter | solution.py:42
  107.6 1.7 copy-start.1
  109.1 4.0 copy-start.4
  109.1 2.6 copy-start.5
  110.1 2.9 copy-start.3
  113.0 0.8 copy-start.6
  116.3 87.1 %reduce-scatter.5.cloned.1.call-start = ((), (), s32[]{:S(2)}) async-start(), calls=%async_computation.7 | async-start | bytes 2949120 | tf_op jit(solution)/shard_map/reduce_scatter | solution.py:42
  159.0 46.3 %all-to-all-start.2 = ((bf16[32,2,1280]{2,1,0:T(2,128)(2,1)}), bf16[32,2,1280]{2,1,0:T(2,128)(2,1)S(1)}, u32[]{:S(2)}, u32[]{:S(2)}) async-start(bf16[32,2,1280]{2,1,0:T(2,128)(2,1)} %copy.35), calls=%async_computation.3 | async-start | bytes 327680 | tf_op jit(solution)/shard_map/all_to_all | solution.py:45
  170.1 46.5 %copy-start.2 = (bf16[256,1280]{1,0:T(8,128)(2,1)S(1)}, bf16[256,1280]{1,0:T(8,128)(2,1)}, u32[]{:S(2)}) copy-start(bf16[256,1280]{1,0:T(8,128)(2,1)} %param.5) | copy-start | bytes 1966084
  205.3 10.4 %copy-start.8 = (bf16[32,2,1280]{2,1,0:T(2,128)(2,1)}, bf16[32,2,1280]{2,1,0:T(2,128)(2,1)S(1)}, u32[]{:S(2)}) copy-start(bf16[32,2,1280]{2,1,0:T(2,128)(2,1)S(1)} %all-to-all-done.2) | copy-start | bytes 491524
  205.3 21.8 %all-to-all-start.3 = ((bf16[32,2,1280]{2,1,0:T(2,128)(2,1)}), bf16[32,2,1280]{2,1,0:T(2,128)(2,1)}, u32[]{:S(2)}, u32[]{:S(2)}) async-start(bf16[32,2,1280]{2,1,0:T(2,128)(2,1)} %copy.36), calls=%async_computation.5 | async-start | bytes 327680 | tf_op jit(solution)/shard_map/all_to_all | solution.py:45
  215.6 260.7 %all-reduce.2.cloned.1.call-start = ((), (), s32[]{:S(2)}) async-start(), calls=%async_computation.8 | async-start | bytes 655360 | tf_op jit(solution)/shard_map/psum | solution.py:99
  219.1 13.6 %copy-start.7 = (bf16[1280,64]{0,1:T(8,128)(2,1)S(1)}, bf16[1280,64]{0,1:T(8,128)(2,1)}, u32[]{:S(2)}) copy-start(bf16[1280,64]{0,1:T(8,128)(2,1)} %param.6) | copy-start | bytes 491524
  230.3 0.6 copy-start.9
Sparse Core Ops, SparseCore 0:
  55.3 13.8 all-gather.6
  89.5 17.9 all-gather.4
  116.4 40.7 reduce-scatter.2
  159.6 43.8 reduce-scatter.4
  232.9 243.3 all-reduce.1
where the time goes:
time: 485 us
  waiting for transfers between devices  326 us (67%)
  blocking collectives  70.8 us (15%)
  matrix products  30 us (6%)
  starting transfers between devices  21.7 us (4%)
  local copies, waits for them, and re-layouts  16.6 us (3%)
  between operations  14 us (3%)
  other arithmetic  5.36 us (1%)
    psum x1, waiting for transfers between devices, local(): router_grad = lax.psum(router_part, DP_EXPERT)  241 us
    reduce_scatter x2, waiting for transfers between devices, to_owners(): lax.psum_scatter(partial_value, DP, scatter_dimension=0, tiled=True)  61.7 us
    all_to_all x2, blocking collectives, to_experts(): lax.all_to_all(slot_rows, 'expert', split_axis=1, concat_axis=0, tiled=True)  40.8 us
    all_gather x2, blocking collectives, gather_in_order(): blocks = lax.all_gather(blocks, axes[k])  30 us
    all_to_all x2, starting transfers between devices, to_owners(): lax.all_to_all(summed, 'expert', split_axis=0, concat_axis=1, tiled=True)  21.5 us
    all_gather x2, waiting for transfers between devices, gather_in_order(): blocks = lax.all_gather(blocks, axes[k])  15.6 us
  transfers between devices with their start and end apart: 7, of which 5 were waited for; matrix products, arithmetic and copies ran while one was open for 6% of the time, Pallas kernels for 0%

commit v1 on v0

--- a/solution.py
+++ b/solution.py
@@ -96,7 +96,7 @@
         "bme,de->bmd", logit_b, router, preferred_element_type=jnp.float32
     )
     router_part = jnp.einsum("bmd,bme->de", inputs, logit_b, preferred_element_type=jnp.float32)
-    router_grad = lax.psum(router_part, DP_EXPERT)
+    router_grad = lax.psum(lax.psum(router_part, "dp_0"), ("dp_1", "expert"))
     return (
         token_grad.astype(jnp.bfloat16).reshape(images * M, feature),
         router_grad,

time: 485 us -> 1090 us (2.25); the launches traced: 485 us -> 1070 us
  waiting for transfers between devices: 326 us -> 916 us
    psum x1 -> x2, waiting for transfers between devices: 241 us -> 825 us  [local(): router_grad = lax.psum(lax.psum(router_part, 'dp_0'), ('dp_1', 'expert'))]
  transfers between devices with their start and end apart: 7 -> 8, of which waited for: 5 -> 6; matrix products, arithmetic and copies ran while one was open for 6% -> 2% of each run, Pallas kernels for 0% -> 0%
where the time goes in v1:
time: 1090 us; the launch traced here: 1070 us
  waiting for transfers between devices  916 us (84%)
  blocking collectives  70.8 us (6%)
  matrix products  27.5 us (3%)
  starting transfers between devices  21.8 us (2%)
  local copies, waits for them, and re-layouts  17.2 us (2%)
  between operations  14.4 us (1%)
    psum x2, waiting for transfers between devices, local(): router_grad = lax.psum(lax.psum(router_part, 'dp_0'), ('dp_1', 'expert'))  825 us
    reduce_scatter x2, waiting for transfers between devices, to_owners(): lax.psum_scatter(partial_value, DP, scatter_dimension=0, tiled=True)  70.2 us
    all_to_all x2, blocking collectives, to_experts(): lax.all_to_all(slot_rows, 'expert', split_axis=1, concat_axis=0, tiled=True)  40.8 us
    all_gather x2, blocking collectives, gather_in_order(): blocks = lax.all_gather(blocks, axes[k])  30 us
  transfers between devices with their start and end apart: 8, of which 6 were waited for; matrix products, arithmetic and copies ran while one was open for 2% of the time, Pallas kernels for 0%

profile of v1, /device:TPU:1, one launch (start us, length us, event | category | flops | bytes accessed | tf_op | source)
XLA Modules:
  0.0 1073.2 jit_solution(10684066237586223130)
XLA Ops:
  7.2 0.0 all-gather.7.cloned.1.call-start
  7.2 1.7 fusion.21
  9.0 0.2 fusion.13
  9.2 1.4 fusion.2
  10.5 0.3 copy.45
  10.8 0.5 broadcast.53
  11.3 1.6 reduce.16
  12.9 0.1 reshape.119
  13.0 25.8 %all_to_all.42 = bf16[32,2,1280]{2,1,0:T(2,128)(2,1)S(1)} all-to-all(bf16[32,2,1280]{2,1,0:T(2,128)(2,1)S(1)} %reshape.119), channel_id=1, replica_groups=mesh['dp_0'=4,'dp_1'=2,'expert'=32] {'expert'}, dimensions={0} | all-to-all | bytes 327680 | tf_op jit(solution)/shard_map/all_to_all | solution.py:37
  38.8 0.1 reshape.120
  38.9 0.9 bitcast_reduce_fusion.1
  39.8 0.1 all_to_all.15
  39.9 15.2 %all_gather.23 = bf16[4,32,2,1280]{3,1,2,0:T(8,128)(2,1)} all-gather(bf16[1,32,2,1280]{3,1,2,0:T(8,128)(2,1)S(1)} %copy.33), channel_id=1, replica_groups=mesh['dp_0'=4,'dp_1'=2,'expert'=32] {'dp_0'}, dimensions={0}, use_global_device_ids=true | all-gather | bytes 819200 | tf_op jit(solution)/shard_map/all_gather | solution.py:21
  55.2 0.0 all-gather.7.cloned.1.call-update
  55.2 0.0 all-gather.5.cloned.1.call-start
  55.3 1.3 fusion.1
  56.6 0.3 copy.46
  56.8 1.6 reduce.17
  58.4 0.1 reshape.121
  58.5 15.0 %all_to_all.43 = bf16[32,2,1280]{2,1,0:T(2,128)(2,1)S(1)} all-to-all(bf16[32,2,1280]{2,1,0:T(2,128)(2,1)S(1)} %reshape.121), channel_id=1, replica_groups=mesh['dp_0'=4,'dp_1'=2,'expert'=32] {'expert'}, dimensions={0} | all-to-all | bytes 327680 | tf_op jit(solution)/shard_map/all_to_all | solution.py:37
  73.5 0.1 reshape.122
  73.6 0.9 bitcast_reduce_fusion
  74.5 0.1 all_to_all.13
  74.6 14.8 %all_gather.20 = bf16[4,32,2,1280]{3,1,2,0:T(8,128)(2,1)} all-gather(bf16[1,32,2,1280]{3,1,2,0:T(8,128)(2,1)S(1)} %copy.30), channel_id=1, replica_groups=mesh['dp_0'=4,'dp_1'=2,'expert'=32] {'dp_0'}, dimensions={0}, use_global_device_ids=true | all-gather | bytes 819200 | tf_op jit(solution)/shard_map/all_gather | solution.py:21
  89.4 0.0 all-gather.5.cloned.1.call-update
  89.4 0.0 reduce-scatter.3.cloned.1.call-start
  89.5 0.0 all-gather.7.cloned.1.call-done
  89.5 2.5 copy.34
  92.0 15.6 %all-gather.5.cloned.1.call-done = bf16[8,32,2,1280]{3,1,2,0:T(8,128)(2,1)} async-done(((bf16[4,32,2,1280]{3,1,2,0:T(8,128)(2,1)}), bf16[8,32,2,1280]{3,1,2,0:T(8,128)(2,1)}) %all-gather.5.cloned.1.call-update) | async-done | bytes 1310736 | tf_op jit(solution)/shard_map/all_gather | solution.py:21
  107.6 1.5 copy.31
  109.1 0.2 copy-done.1
  109.3 0.8 convolution_bitcast_fusion.3
  110.1 1.6 copy-done.5
  111.7 1.3 fusion.9
  113.1 0.8 copy-done.6
  113.8 2.4 convolution_bitcast_fusion.1
  116.2 0.0 reduce-scatter.3.cloned.1.call-update
  116.3 0.0 reduce-scatter.5.cloned.1.call-start
  116.3 4.4 convolution_bitcast_fusion
  120.8 36.4 %reduce-scatter.3.cloned.1.call-done = f32[32,2,1280]{2,0,1:T(8,128)} async-done(((f32[256,2,1280]{2,0,1:T(8,128)}), f32[32,2,1280]{2,0,1:T(8,128)}) %reduce-scatter.3.cloned.1.call-update) | async-done | bytes 327696 | tf_op jit(solution)/shard_map/reduce_scatter | solution.py:42
  157.2 1.0 convert_element_type.53
  158.2 0.8 copy.35
  159.0 10.9 %all-to-all-start.2 = ((bf16[32,2,1280]{2,1,0:T(2,128)(2,1)}), bf16[32,2,1280]{2,1,0:T(2,128)(2,1)S(1)}, u32[]{:S(2)}, u32[]{:S(2)}) async-start(bf16[32,2,1280]{2,1,0:T(2,128)(2,1)} %copy.35), calls=%async_computation.3 | async-start | bytes 327680 | tf_op jit(solution)/shard_map/all_to_all | solution.py:45
  169.9 33.9 %reduce-scatter.5.cloned.1.call-done = f32[32,2,1280]{2,0,1:T(8,128)} async-done(((f32[256,2,1280]{2,0,1:T(8,128)}), f32[32,2,1280]{2,0,1:T(8,128)}) %reduce-scatter.5.cloned.1.call-update) | async-done | bytes 327696 | tf_op jit(solution)/shard_map/reduce_scatter | solution.py:42
  203.8 1.0 convert_element_type.55
  204.8 0.8 copy.36
  205.6 0.7 copy-done.8
  206.3 10.4 all-to-all-start.3
  216.7 0.2 all-reduce.3.cloned.1.call-start
  217.0 4.1 convolution_convert_fusion
  221.0 1.0 reshape.113
  222.0 1.0 convolution_bitcast_fusion.5
  223.0 5.1 all-to-all-done.3
  228.1 1.6 reshape.114
  229.8 1.6 multiply_reduce_fusion.1
  231.4 0.6 copy-done.10
  232.0 1.9 convolution_bitcast_fusion.2
  233.9 0.0 all-reduce.5.cloned.1.call-start
  233.9 3.9 convolution_convert_fusion.1
  237.8 42.3 %all-reduce.3.cloned.1.call-done = f32[1280,64]{0,1:T(8,128)} async-done(((f32[1280,64]{0,1:T(8,128)}), f32[1280,64]{0,1:T(8,128)}) %all-reduce.3.cloned.1.call-update) | async-done | bytes 327696 | tf_op jit(solution)/shard_map/psum | solution.py:99
  280.2 0.4 fusion.15
  280.6 1.3 fusion
  281.9 782.7 %all-reduce.5.cloned.1.call-done = f32[1280,64]{0,1:T(8,128)} async-done(((f32[1280,64]{0,1:T(8,128)}), f32[1280,64]{0,1:T(8,128)}) %all-reduce.5.cloned.1.call-update) | async-done | bytes 327696 | tf_op jit(solution)/shard_map/psum | solution.py:99
  1064.6 1.7 copy.51
  (25 shorter events, 0.1 us)
Async XLA Ops:
  7.2 101.9 %copy-start = (bf16[2,1280,512]{2,1,0:T(8,128)(2,1)S(1)}, bf16[2,1280,512]{2,1,0:T(8,128)(2,1)}, u32[]{:S(2)}) copy-start(bf16[2,1280,512]{2,1,0:T(8,128)(2,1)} %param.7) | copy-start | bytes 7864324
  7.2 82.3 %all-gather.7.cloned.1.call-start = ((), (), s32[]{:S(2)}) async-start(), calls=%async_computation.11 | async-start | bytes 1966080 | tf_op jit(solution)/shard_map/all_gather | solution.py:21
  55.2 52.3 %all-gather.5.cloned.1.call-start = ((), (), s32[]{:S(2)}) async-start(), calls=%async_computation.10 | async-start | bytes 1966080 | tf_op jit(solution)/shard_map/all_gather | solution.py:21
  89.4 67.8 %reduce-scatter.3.cloned.1.call-start = ((), (), s32[]{:S(2)}) async-start(), calls=%async_computation.6 | async-start | bytes 2949120 | tf_op jit(solution)/shard_map/reduce_scatter | solution.py:42
  107.6 1.7 copy-start.1
  109.1 4.0 copy-start.4
  109.1 2.6 copy-start.5
  110.1 2.9 copy-start.3
  113.0 0.8 copy-start.6
  116.3 87.5 %reduce-scatter.5.cloned.1.call-start = ((), (), s32[]{:S(2)}) async-start(), calls=%async_computation.7 | async-start | bytes 2949120 | tf_op jit(solution)/shard_map/reduce_scatter | solution.py:42
  159.0 46.6 %all-to-all-start.2 = ((bf16[32,2,1280]{2,1,0:T(2,128)(2,1)}), bf16[32,2,1280]{2,1,0:T(2,128)(2,1)S(1)}, u32[]{:S(2)}, u32[]{:S(2)}) async-start(bf16[32,2,1280]{2,1,0:T(2,128)(2,1)} %copy.35), calls=%async_computation.3 | async-start | bytes 327680 | tf_op jit(solution)/shard_map/all_to_all | solution.py:45
  205.6 0.7 copy-start.8
  206.3 21.8 %all-to-all-start.3 = ((bf16[32,2,1280]{2,1,0:T(2,128)(2,1)}), bf16[32,2,1280]{2,1,0:T(2,128)(2,1)}, u32[]{:S(2)}, u32[]{:S(2)}) async-start(bf16[32,2,1280]{2,1,0:T(2,128)(2,1)} %copy.36), calls=%async_computation.5 | async-start | bytes 327680 | tf_op jit(solution)/shard_map/all_to_all | solution.py:45
  216.7 5.3 copy-start.2
  216.7 63.4 %all-reduce.3.cloned.1.call-start = ((), (), s32[]{:S(2)}) async-start(), calls=%async_computation.8 | async-start | bytes 655360 | tf_op jit(solution)/shard_map/psum | solution.py:99
  231.4 0.6 copy-start.10
  233.9 46.8 %copy-start.7 = (bf16[1280,64]{0,1:T(8,128)(2,1)S(1)}, bf16[1280,64]{0,1:T(8,128)(2,1)}, u32[]{:S(2)}) copy-start(bf16[1280,64]{0,1:T(8,128)(2,1)} %param.6) | copy-start | bytes 491524
  233.9 46.8 %copy-start.9 = (f32[256,64]{0,1:T(8,128)S(1)}, f32[256,64]{0,1:T(8,128)}, u32[]{:S(2)}) copy-start(f32[256,64]{0,1:T(8,128)} %convolution_bitcast_fusion.5) | copy-start | bytes 196612
  233.9 46.8 %copy-start.11 = (f32[256,64]{0,1:T(8,128)S(1)}, f32[256,64]{0,1:T(8,128)}, u32[]{:S(2)}) copy-start(f32[256,64]{0,1:T(8,128)} %copy-done.10) | copy-start | bytes 196612
  233.9 830.7 %all-reduce.5.cloned.1.call-start = ((), (), s32[]{:S(2)}) async-start(), calls=%async_computation.9 | async-start | bytes 655360 | tf_op jit(solution)/shard_map/psum | solution.py:99
Sparse Core Ops, SparseCore 0:
  55.3 13.8 all-gather.6
  89.5 17.9 all-gather.4
  116.4 40.7 reduce-scatter.2
  160.1 43.6 reduce-scatter.4
  234.0 46.1 all-reduce.2
  282.6 781.9 all-reduce.4
